TPU v7x, 512 devices: a whole 4x4x16 slice. The times are simulated.
512 devices in a mesh: grp: 8 (over y, core), dev: 64 (over z, x).
Axes of the slice: x: 4, y: 4, z: 16, core: 2. Of those that a mesh axis runs over, the one named last changes fastest.
Arguments:
- right_side: float32 [512, 8192], P('grp', 'dev'), may hold values from -6 to 6
- previous: float32 [512, 8192], P('grp', 'dev'), may hold values from -4 to 4
- east_face: float32 [512, 8192], P('grp', 'dev'), may hold values from 0.5 to 10
- south_face: float32 [512, 8192], P('grp', 'dev'), may hold values from 0.5 to 10
- wet_mask: int32 [512, 8192], P('grp', 'dev'), may hold values from 0 to 1, as said below
Outputs:
- surface: float32 [512, 8192], P('grp', 'dev')
- residual: float32 [512, 8192], P('grp', 'dev')
Inputs may be any that keep to these rules, and one draw needn't show every extreme that they name: `wet_mask`: dry cells form axis-aligned rectangles of 1 to 7 by 1 to 7 cells; each lies inside one aligned tile of 16 x 16 cells, one cell or more away from the tile's border, at most one rectangle a tile.
All inputs are finite; a program needn't handle non-finite values.
Results may differ from a plain program's by a relative error of at most 0.0003.
Values sent between devices are 32-bit elements; how exact they have to be, the bound alone decides.
No kernel may reach another device: no remote copies, remote signals or barrier semaphores. Data moves between devices by JAX's collectives and lax.ppermute only.
A program may use at most 64 MiB of HBM per device.

v0:
```python
import jax
import jax.numpy as jnp
from jax import lax
from jax.sharding import PartitionSpec as P

CYCLES = 2
PRE = 2
POST = 2
COARSE_SWEEPS = 4
relax_weight = 0.8
wet_mass = 2e-05


def extended_2(value, sides, width):
    for axis, dim in sides:
        peers, length = (lax.axis_size(axis), value.shape[dim])
        up = [(i, (i + 1) % peers) for i in range(peers - 1)]
        down = [(j, i) for i, j in up]
        last = lax.slice_in_dim(value, length - width, length, axis=dim)
        initial = lax.slice_in_dim(value, 0, width, axis=dim)
        before = lax.ppermute(last, axis, up)
        after = lax.ppermute(initial, axis, down)
        value = jnp.concatenate([before, value, after], axis=dim)
    return value


def coarsen_sum(values):
    row_count, col_count = values.shape
    return values.reshape(row_count // 2, 2, col_count // 2, 2).sum(axis=(1, 3))


def coarsen_links(coefficients):
    mass_term, east_link, west_link, south_link, north_link = coefficients
    return (
        coarsen_sum(mass_term),
        east_link[0::2, 1::2] + east_link[1::2, 1::2],
        west_link[0::2, 0::2] + west_link[1::2, 0::2],
        south_link[1::2, 0::2] + south_link[1::2, 1::2],
        north_link[0::2, 0::2] + north_link[0::2, 1::2],
    )


def inverse_diagonal(coefficients):
    mass_term, east_link, west_link, south_link, north_link = coefficients
    return 1.0 / (mass_term + east_link + west_link + south_link + north_link)


def operate(padded, coefficients):
    mass_term, east_link, west_link, south_link, north_link = coefficients
    centre = padded[1:-1, 1:-1]
    return (
        mass_term * centre
        + east_link * (centre - padded[1:-1, 2:])
        + west_link * (centre - padded[1:-1, :-2])
        + south_link * (centre - padded[2:, 1:-1])
        + north_link * (centre - padded[:-2, 1:-1])
    )


def jacobi_sweep(values, padded, source, coefficients, inverse):
    return values + relax_weight * (source - operate(padded, coefficients)) * inverse


def zero_padded(values):
    return jnp.pad(values, 1)


def block_padded(values):
    return extended_2(values, (("grp", 0), ("dev", 1)), 1)


def strip_padded(values):
    row_padded = extended_2(values, (("grp", 0),), 1)
    return jnp.pad(row_padded, ((0, 0), (1, 1)))


def prolong(values):
    return jnp.repeat(jnp.repeat(values, 2, axis=0), 2, axis=1)


def smoothing(values, source, coefficients, inverse, sweeps, from_zero, padder):
    for sweep_index in range(sweeps):
        if from_zero and sweep_index == 0:
            values = relax_weight * source * inverse
        else:
            values = jacobi_sweep(values, padder(values), source, coefficients, inverse)
    return values


def unstack(stacked):
    return tuple((stacked[position] for position in range(5)))


def shards(right_side, previous, east_face, south_face, wet_mask):
    group_index = lax.axis_index("grp")
    member_index = lax.axis_index("dev")
    wet = wet_mask.astype(jnp.float32)
    extended = extended_2(jnp.stack([wet, east_face, south_face]), (("grp", 1), ("dev", 2)), 1)
    wet_pad = extended[0]
    east_pad = extended[1]
    south_pad = extended[2]
    east_link = east_face * wet * wet_pad[1:-1, 2:]
    west_link = east_pad[1:-1, :-2] * wet_pad[1:-1, :-2] * wet
    south_link = south_face * wet * wet_pad[2:, 1:-1]
    north_link = south_pad[:-2, 1:-1] * wet_pad[:-2, 1:-1] * wet
    mass_term = wet * wet_mass + (1.0 - wet)
    source = wet * right_side + (1.0 - wet) * previous
    hierarchy = [(mass_term, east_link, west_link, south_link, north_link)]
    for level_index in range(3):
        hierarchy.append(coarsen_links(hierarchy[-1]))
    inverses = [inverse_diagonal(coefficients) for coefficients in hierarchy]
    strip_coefficients = unstack(lax.all_gather(jnp.stack(hierarchy[3]), "dev", axis=2, tiled=True))
    strip_inverse = inverse_diagonal(strip_coefficients)
    coarse_coefficients = coarsen_links(strip_coefficients)
    whole_coefficients = unstack(
        lax.all_gather(jnp.stack(coarse_coefficients), "grp", axis=1, tiled=True)
    )
    whole_inverse = inverse_diagonal(whole_coefficients)
    whole_mass = jnp.sum(whole_coefficients[0])

    def coarse_level(local_source):
        strip_source = lax.all_gather(local_source, "dev", axis=1, tiled=True)
        strip_values = smoothing(
            None, strip_source, strip_coefficients, strip_inverse, PRE, True, strip_padded
        )
        strip_rest = coarsen_sum(
            strip_source - operate(strip_padded(strip_values), strip_coefficients)
        )
        strip_rows = strip_rest.shape[0]
        whole_source = lax.all_gather(strip_rest, "grp", axis=0, tiled=True)
        whole_values = smoothing(
            None, whole_source, whole_coefficients, whole_inverse, COARSE_SWEEPS, True, zero_padded
        )
        whole_rest = whole_source - operate(zero_padded(whole_values), whole_coefficients)
        shift_value = relax_weight * jnp.sum(whole_rest) / whole_mass
        coarse_values = lax.dynamic_slice_in_dim(
            whole_values, group_index * strip_rows, strip_rows, 0
        )
        coarse_values = coarse_values + shift_value
        strip_values = strip_values + prolong(coarse_values)
        strip_values = smoothing(
            strip_values, strip_source, strip_coefficients, strip_inverse, POST, False, strip_padded
        )
        local_width = local_source.shape[1]
        return lax.dynamic_slice_in_dim(strip_values, member_index * local_width, local_width, 1)

    def descend(level_index, values, level_source, from_zero):
        if level_index == 3:
            return coarse_level(level_source)
        coefficients = hierarchy[level_index]
        values = smoothing(
            values, level_source, coefficients, inverses[level_index], PRE, from_zero, block_padded
        )
        remainder = coarsen_sum(level_source - operate(block_padded(values), coefficients))
        values = values + prolong(descend(level_index + 1, None, remainder, True))
        return smoothing(
            values, level_source, coefficients, inverses[level_index], POST, False, block_padded
        )

    surface = previous
    for cycle_index in range(CYCLES):
        surface = descend(0, surface, source, False)
    residual = source - operate(block_padded(surface), hierarchy[0])
    return (surface, residual)


def solution(mesh):
    placed = (P("grp", "dev"), P("grp", "dev"), P("grp", "dev"), P("grp", "dev"), P("grp", "dev"))
    return jax.shard_map(
        shards,
        mesh=mesh,
        in_specs=placed,
        out_specs=(P("grp", "dev"), P("grp", "dev")),
        check_vma=False,
    )
```

profile of v0, /device:TPU:129, one launch (start us, length us, event | category | flops | bytes accessed | tf_op | source)
XLA Modules:
  0.0 903.5 jit_solution(13340431999990689571)
XLA Ops:
  21.1 5.5 collective-permute-start.3
  78.6 4.8 collective-permute-start.16
  117.8 81.8 %all_gather.19 = f32[5,8,1024]{1,0,2:T(8,128)S(1)} all-gather(f32[5,8,16]{1,0,2:T(8,128)S(1)} %copy.45), channel_id=1, replica_groups=mesh['grp'=8,'dev'=64] {'dev'}, dimensions={2}, use_global_device_ids=true | all-gather | bytes 166400 | tf_op jit(solution)/shard_map/all_gather | solution.py:112
  208.2 25.2 %collective-permute-start.24 = (f32[1,32]{1,0:T(1,128)S(1)}, f32[1,32]{1,0:T(1,128)S(1)}, u32[]{:S(2)}, u32[]{:S(2)}) collective-permute-start(f32[1,32]{1,0:T(1,128)S(1)} %get-tuple-element.169), channel_id=1, source_target_pairs={{0,64},{64,128},{128,192},{192,256},{256,320},{320,384},{384,448},... | collective-permute-start | bytes 392 | tf_op jit(solution)/shard_map/ppermute | solution.py:21
  244.6 5.8 collective-permute-done.27
  264.2 4.4 collective-permute-done.31
  268.9 59.9 %all-gather = f32[64,16,8]{1,2,0:T(8,128)S(1)} all-gather(f32[1,16,8]{1,2,0:T(8,128)S(1)} %bitcast.353), channel_id=1, replica_groups=mesh['grp'=8,'dev'=64] {'dev'}, dimensions={0}, use_global_device_ids=true | all-gather | bytes 33280 | tf_op jit(solution)/shard_map/all_gather | solution.py:122
  329.1 21.8 %collective-permute-start.32 = (f32[1,1024]{1,0:T(1,128)S(1)}, f32[1,1024]{1,0:T(1,128)S(1)}, u32[]{:S(2)}, u32[]{:S(2)}) collective-permute-start(f32[1,1024]{1,0:T(1,128)S(1)} %get-tuple-element.97), channel_id=1, source_target_pairs={{0,64},{64,128},{128,192},{192,256},{256,320},{320,384},{384,448},... | collective-permute-start | bytes 12296 | tf_op jit(solution)/shard_map/ppermute | solution.py:21
  352.8 14.5 %all_gather.21 = f32[5,32,512]{2,0,1:T(8,128)S(1)} all-gather(f32[5,4,512]{2,0,1:T(8,128)S(1)} %copy.51), channel_id=1, replica_groups=mesh['grp'=8,'dev'=64] {'grp'}, dimensions={1}, use_global_device_ids=true | all-gather | bytes 368640 | tf_op jit(solution)/shard_map/all_gather | solution.py:116
  377.4 11.2 %all-gather.1 = f32[8,4,512]{2,1,0:T(4,128)S(1)} all-gather(f32[1,4,512]{2,1,0:T(4,128)S(1)} %bitcast.350), channel_id=1, replica_groups=mesh['grp'=8,'dev'=64] {'grp'}, dimensions={0}, use_global_device_ids=true | all-gather | bytes 73728 | tf_op jit(solution)/shard_map/all_gather | solution.py:130
  420.8 5.8 collective-permute-done.43
  458.6 4.5 collective-permute-done.51
  476.7 4.5 collective-permute-done.55
  494.9 4.6 collective-permute-done.59
  513.3 4.6 collective-permute-done.63
  531.4 4.6 collective-permute-done.67
  549.6 4.6 collective-permute-done.71
  567.7 4.6 collective-permute-done.75
  588.4 4.5 collective-permute-done.79
  606.3 4.5 collective-permute-done.83
  625.0 4.4 collective-permute-done.87
  642.9 4.4 collective-permute-done.91
  647.6 60.0 %all-gather.2 = f32[64,16,8]{1,2,0:T(8,128)S(1)} all-gather(f32[1,16,8]{1,2,0:T(8,128)S(1)} %bitcast.354), channel_id=1, replica_groups=mesh['grp'=8,'dev'=64] {'dev'}, dimensions={0}, use_global_device_ids=true | all-gather | bytes 33280 | tf_op jit(solution)/shard_map/all_gather | solution.py:122
  707.8 21.8 %collective-permute-start.92 = (f32[1,1024]{1,0:T(1,128)S(1)}, f32[1,1024]{1,0:T(1,128)S(1)}, u32[]{:S(2)}, u32[]{:S(2)}) collective-permute-start(f32[1,1024]{1,0:T(1,128)S(1)} %get-tuple-element.76), channel_id=1, source_target_pairs={{0,64},{64,128},{128,192},{192,256},{256,320},{320,384},{384,448},... | collective-permute-start | bytes 12296 | tf_op jit(solution)/shard_map/ppermute | solution.py:21
  744.3 11.2 %all-gather.3 = f32[8,4,512]{2,1,0:T(4,128)S(1)} all-gather(f32[1,4,512]{2,1,0:T(4,128)S(1)} %bitcast.349), channel_id=1, replica_groups=mesh['grp'=8,'dev'=64] {'grp'}, dimensions={0}, use_global_device_ids=true | all-gather | bytes 73728 | tf_op jit(solution)/shard_map/all_gather | solution.py:130
  787.4 5.8 collective-permute-done.103
  807.0 4.4 collective-permute-done.107
  825.1 4.5 collective-permute-done.111
  843.3 4.5 collective-permute-done.115
  861.5 4.6 collective-permute-done.119
  879.8 4.6 collective-permute-done.123
  898.0 4.6 collective-permute-done.127
  (535 shorter events, 480.6 us)
Async XLA Ops:
  1.4 12.8 %collective-permute-start.4 = (f32[1,128]{1,0:T(1,128)S(1)}, f32[1,128]{1,0:T(1,128)S(1)}, u32[]{:S(2)}, u32[]{:S(2)}) collective-permute-start(f32[1,128]{1,0:T(1,128)S(1)} %get-tuple-element.105), channel_id=1, source_target_pairs={{0,64},{64,128},{128,192},{192,256},{256,320},{320,384},{384,448},... | collective-permute-start | bytes 1544 | tf_op jit(solution)/shard_map/ppermute | solution.py:21
  5.1 9.0 collective-permute-start.5
  18.0 14.0 %collective-permute-start.2 = (f32[3,66,1]{2,1,0:T(8,128)S(1)}, f32[3,66,1]{2,1,0:T(8,128)S(1)}, u32[]{:S(2)}, u32[]{:S(2)}) collective-permute-start(f32[3,66,1]{2,1,0:T(8,128)S(1)} %get-tuple-element.34), channel_id=1, source_target_pairs={{0,1},{1,2},{2,3},{3,4},{4,5},{5,6},{6,7},{7,8},{8,9},{9,10},{10,1... | collective-permute-start | bytes 2384 | tf_op jit(solution)/shard_map/ppermute | solution.py:21
  21.1 10.9 %collective-permute-start.3 = (f32[3,66,1]{2,1,0:T(8,128)S(1)}, f32[3,66,1]{2,1,0:T(8,128)S(1)}, u32[]{:S(2)}, u32[]{:S(2)}) collective-permute-start(f32[3,66,1]{2,1,0:T(8,128)S(1)} %get-tuple-element.35), channel_id=1, source_target_pairs={{1,0},{2,1},{3,2},{4,3},{5,4},{6,5},{7,6},{8,7},{9,8},{10,9},{11,1... | collective-permute-start | bytes 2384 | tf_op jit(solution)/shard_map/ppermute | solution.py:22
  28.6 8.0 collective-permute-start.7
  48.5 8.0 collective-permute-start.11
  56.7 9.3 %collective-permute-start.12 = (f32[1,128]{1,0:T(1,128)S(1)}, f32[1,128]{1,0:T(1,128)S(1)}, u32[]{:S(2)}, u32[]{:S(2)}) collective-permute-start(f32[1,128]{1,0:T(1,128)S(1)} %get-tuple-element.101), channel_id=1, source_target_pairs={{0,64},{64,128},{128,192},{192,256},{256,320},{320,384},{384,448},... | collective-permute-start | bytes 1544 | tf_op jit(solution)/shard_map/ppermute | solution.py:21
  68.0 8.0 collective-permute-start.15
  90.3 7.8 collective-permute-start.19
  108.2 7.8 collective-permute-start.23
  208.2 27.2 %collective-permute-start.24 = (f32[1,32]{1,0:T(1,128)S(1)}, f32[1,32]{1,0:T(1,128)S(1)}, u32[]{:S(2)}, u32[]{:S(2)}) collective-permute-start(f32[1,32]{1,0:T(1,128)S(1)} %get-tuple-element.169), channel_id=1, source_target_pairs={{0,64},{64,128},{128,192},{192,256},{256,320},{320,384},{384,448},... | collective-permute-start | bytes 392 | tf_op jit(solution)/shard_map/ppermute | solution.py:21
  242.7 7.8 collective-permute-start.27
  260.8 7.8 collective-permute-start.31
  329.1 38.3 %collective-permute-start.32 = (f32[1,1024]{1,0:T(1,128)S(1)}, f32[1,1024]{1,0:T(1,128)S(1)}, u32[]{:S(2)}, u32[]{:S(2)}) collective-permute-start(f32[1,1024]{1,0:T(1,128)S(1)} %get-tuple-element.97), channel_id=1, source_target_pairs={{0,64},{64,128},{128,192},{192,256},{256,320},{320,384},{384,448},... | collective-permute-start | bytes 12296 | tf_op jit(solution)/shard_map/ppermute | solution.py:21
  350.9 16.4 %collective-permute-start.33 = (f32[1,1024]{1,0:T(1,128)S(1)}, f32[1,1024]{1,0:T(1,128)S(1)}, u32[]{:S(2)}, u32[]{:S(2)}) collective-permute-start(f32[1,1024]{1,0:T(1,128)S(1)} %get-tuple-element.96), channel_id=1, source_target_pairs={{64,0},{128,64},{192,128},{256,192},{320,256},{384,320},{448,384},... | collective-permute-start | bytes 12296 | tf_op jit(solution)/shard_map/ppermute | solution.py:22
  418.9 7.8 collective-permute-start.43
  455.2 7.8 collective-permute-start.51
  473.3 7.8 collective-permute-start.55
  491.5 8.0 collective-permute-start.59
  509.9 8.0 collective-permute-start.63
  528.0 8.0 collective-permute-start.67
  546.2 8.0 collective-permute-start.71
  564.4 8.0 collective-permute-start.75
  585.0 7.8 collective-permute-start.79
  603.0 7.8 collective-permute-start.83
  621.6 7.8 collective-permute-start.87
  707.8 23.7 %collective-permute-start.92 = (f32[1,1024]{1,0:T(1,128)S(1)}, f32[1,1024]{1,0:T(1,128)S(1)}, u32[]{:S(2)}, u32[]{:S(2)}) collective-permute-start(f32[1,1024]{1,0:T(1,128)S(1)} %get-tuple-element.76), channel_id=1, source_target_pairs={{0,64},{64,128},{128,192},{192,256},{256,320},{320,384},{384,448},... | collective-permute-start | bytes 12296 | tf_op jit(solution)/shard_map/ppermute | solution.py:21
  821.8 7.8 collective-permute-start.111
  839.9 7.8 collective-permute-start.115
  858.1 8.0 collective-permute-start.119
  876.4 8.0 collective-permute-start.123
  894.6 8.0 collective-permute-start.127
  (108 other events, 1214.5 us)
where the time goes:
time: 914 us; the launch traced here: 904 us
  starting transfers between devices  397 us (43%)
  blocking collectives  239 us (26%)
  waiting for transfers between devices  214 us (23%)
  local copies, waits for them, and re-layouts  30.7 us (3%)
  other arithmetic  16.4 us (2%)
    ppermute x64, starting transfers between devices, extended_2(): before = lax.ppermute(last, axis, up)  261 us
    ppermute x64, starting transfers between devices, extended_2(): after = lax.ppermute(initial, axis, down)  136 us
    ppermute x64, waiting for transfers between devices, extended_2(): before = lax.ppermute(last, axis, up)  123 us
    all_gather x2, blocking collectives, coarse_level(): strip_source = lax.all_gather(local_source, 'dev', axis=1, tiled=True)  120 us
    ppermute x64, waiting for transfers between devices, extended_2(): after = lax.ppermute(initial, axis, down)  91.4 us
    all_gather x1, blocking collectives, shards(): lax.all_gather(jnp.stack(hierarchy[3]), 'dev', axis=2, tiled=True)  81.8 us
    all_gather x2, blocking collectives, coarse_level(): whole_source = lax.all_gather(strip_rest, 'grp', axis=0, tiled=True)  22.4 us
  transfers between devices with their start and end apart: 128, of which 60 were waited for; matrix products, arithmetic and copies ran while one was open for 1% of the time, Pallas kernels for 0%

commit v1 on v0

--- a/solution.py
+++ b/solution.py
@@ -119,7 +119,15 @@
     whole_mass = jnp.sum(whole_coefficients[0])
 
     def coarse_level(local_source):
-        strip_source = lax.all_gather(local_source, "dev", axis=1, tiled=True)
+        strip_source = jnp.concatenate(
+            lax.all_to_all(
+                jnp.stack([local_source] * lax.axis_size("dev")),
+                axis_name="dev",
+                split_axis=0,
+                concat_axis=0,
+            ),
+            axis=1,
+        )
         strip_values = smoothing(
             None, strip_source, strip_coefficients, strip_inverse, PRE, True, strip_padded
         )

time: 914 us -> 801 us (0.88)
  blocking collectives: 239 us -> 135 us
  starting transfers between devices: 397 us -> 375 us
  waiting for transfers between devices: 214 us -> 224 us
    all_gather x2 -> x0, blocking collectives: 120 us -> none  [coarse_level(): strip_source = lax.all_gather(local_source, 'dev', axis=1, tiled=True)]
    ppermute x64, starting transfers between devices: 261 us -> 226 us  [extended_2(): before = lax.ppermute(last, axis, up)]
    all_to_all x0 -> x1, blocking collectives: none -> 16.2 us  [coarse_level(): lax.all_to_all(jnp.stack([local_source] * lax.axis_size('dev')), axis_nam...]
    all_to_all x0 -> x1, starting transfers between devices: none -> 11.3 us  [coarse_level(): lax.all_to_all(jnp.stack([local_source] * lax.axis_size('dev')), axis_nam...]
  transfers between devices with their start and end apart: 128 -> 129, of which waited for: 60 -> 61; matrix products, arithmetic and copies ran while one was open for 1% -> 2% of each run, Pallas kernels for 0% -> 0%
where the time goes in v1:
time: 801 us; the launch traced here: 790 us
  starting transfers between devices  375 us (47%)
  waiting for transfers between devices  224 us (28%)
  blocking collectives  135 us (17%)
  local copies, waits for them, and re-layouts  32.4 us (4%)
  other arithmetic  17.7 us (2%)
    ppermute x64, starting transfers between devices, extended_2(): before = lax.ppermute(last, axis, up)  226 us
    ppermute x64, starting transfers between devices, extended_2(): after = lax.ppermute(initial, axis, down)  137 us
    ppermute x64, waiting for transfers between devices, extended_2(): before = lax.ppermute(last, axis, up)  123 us
    ppermute x64, waiting for transfers between devices, extended_2(): after = lax.ppermute(initial, axis, down)  91.4 us
    all_gather x1, blocking collectives, shards(): lax.all_gather(jnp.stack(hierarchy[3]), 'dev', axis=2, tiled=True)  82 us
    all_gather x2, blocking collectives, coarse_level(): whole_source = lax.all_gather(strip_rest, 'grp', axis=0, tiled=True)  22.5 us
    all_to_all x1, blocking collectives, coarse_level(): lax.all_to_all(jnp.stack([local_source] * lax.axis_size('dev')), axis_nam...  16.2 us
  transfers between devices with their start and end apart: 129, of which 61 were waited for; matrix products, arithmetic and copies ran while one was open for 2% of the time, Pallas kernels for 0%

profile of v1, /device:TPU:129, one launch (start us, length us, event | category | flops | bytes accessed | tf_op | source)
XLA Modules:
  0.0 789.5 jit_solution(5940830660263661517)
XLA Ops:
  21.1 5.5 collective-permute-start.3
  78.6 4.8 collective-permute-start.16
  117.8 82.0 %all_gather.12 = f32[5,8,1024]{1,0,2:T(8,128)S(1)} all-gather(f32[5,8,16]{1,0,2:T(8,128)S(1)} %copy.40), channel_id=1, replica_groups=mesh['grp'=8,'dev'=64] {'dev'}, dimensions={2}, use_global_device_ids=true | all-gather | bytes 166400 | tf_op jit(solution)/shard_map/all_gather | solution.py:112
  207.7 25.2 %collective-permute-start.24 = (f32[1,32]{1,0:T(1,128)S(1)}, f32[1,32]{1,0:T(1,128)S(1)}, u32[]{:S(2)}, u32[]{:S(2)}) collective-permute-start(f32[1,32]{1,0:T(1,128)S(1)} %get-tuple-element.169), channel_id=1, source_target_pairs={{0,64},{64,128},{128,192},{192,256},{256,320},{320,384},{384,448},... | collective-permute-start | bytes 392 | tf_op jit(solution)/shard_map/ppermute | solution.py:21
  244.1 5.8 collective-permute-done.27
  263.7 4.4 collective-permute-done.31
  269.2 11.3 %all-to-all-start = ((f32[64,1,128]{2,1,0:T(1,128)}), f32[64,1,128]{2,1,0:T(1,128)S(1)}, u32[]{:S(2)}, u32[]{:S(2)}) async-start(f32[64,1,128]{2,1,0:T(1,128)} %reshape.136), calls=%async_computation | async-start | bytes 65536 | tf_op jit(solution)/shard_map/all_to_all | solution.py:123
  280.5 9.1 %all-to-all-done = f32[64,1,128]{2,1,0:T(1,128)S(1)} async-done(((f32[64,1,128]{2,1,0:T(1,128)}), f32[64,1,128]{2,1,0:T(1,128)S(1)}, u32[]{:S(2)}, u32[]{:S(2)}) %all-to-all-start) | async-done | bytes 32800 | tf_op jit(solution)/shard_map/all_to_all | solution.py:123
  291.2 4.5 collective-permute-start.32
  297.6 14.0 %all_gather.14 = f32[5,32,512]{2,0,1:T(8,128)S(1)} all-gather(f32[5,4,512]{2,0,1:T(8,128)S(1)} %copy.46), channel_id=1, replica_groups=mesh['grp'=8,'dev'=64] {'grp'}, dimensions={1}, use_global_device_ids=true | all-gather | bytes 368640 | tf_op jit(solution)/shard_map/all_gather | solution.py:116
  322.0 11.1 %all-gather = f32[8,4,512]{2,1,0:T(4,128)S(1)} all-gather(f32[1,4,512]{2,1,0:T(4,128)S(1)} %bitcast.332), channel_id=1, replica_groups=mesh['grp'=8,'dev'=64] {'grp'}, dimensions={0}, use_global_device_ids=true | all-gather | bytes 73728 | tf_op jit(solution)/shard_map/all_gather | solution.py:138
  359.4 4.9 collective-permute-start.42
  366.3 5.8 collective-permute-done.43
  404.0 4.5 collective-permute-done.51
  422.2 4.5 collective-permute-done.55
  440.4 4.6 collective-permute-done.59
  458.7 4.6 collective-permute-done.63
  476.9 4.6 collective-permute-done.67
  495.0 4.6 collective-permute-done.71
  513.2 4.6 collective-permute-done.75
  533.8 4.5 collective-permute-done.79
  551.8 4.5 collective-permute-done.83
  588.3 4.4 collective-permute-done.91
  593.2 16.2 %all_to_all.10 = f32[64,1,128]{2,1,0:T(1,128)S(1)} all-to-all(f32[64,1,128]{2,1,0:T(1,128)S(1)} %reshape.138), channel_id=1, replica_groups=mesh['grp'=8,'dev'=64] {'dev'}, dimensions={0} | all-to-all | bytes 65536 | tf_op jit(solution)/shard_map/all_to_all | solution.py:123
  629.4 11.4 %all-gather.1 = f32[8,4,512]{2,1,0:T(4,128)S(1)} all-gather(f32[1,4,512]{2,1,0:T(4,128)S(1)} %bitcast.331), channel_id=1, replica_groups=mesh['grp'=8,'dev'=64] {'grp'}, dimensions={0}, use_global_device_ids=true | all-gather | bytes 73728 | tf_op jit(solution)/shard_map/all_gather | solution.py:138
  666.5 4.9 collective-permute-start.102
  673.4 5.8 collective-permute-done.103
  711.1 4.5 collective-permute-done.111
  729.2 4.5 collective-permute-done.115
  747.4 4.6 collective-permute-done.119
  765.8 4.6 collective-permute-done.123
  783.9 4.6 collective-permute-done.127
  (545 shorter events, 487.7 us)
Async XLA Ops:
  1.4 12.8 %collective-permute-start.4 = (f32[1,128]{1,0:T(1,128)S(1)}, f32[1,128]{1,0:T(1,128)S(1)}, u32[]{:S(2)}, u32[]{:S(2)}) collective-permute-start(f32[1,128]{1,0:T(1,128)S(1)} %get-tuple-element.105), channel_id=1, source_target_pairs={{0,64},{64,128},{128,192},{192,256},{256,320},{320,384},{384,448},... | collective-permute-start | bytes 1544 | tf_op jit(solution)/shard_map/ppermute | solution.py:21
  5.1 9.0 %collective-permute-start.5 = (f32[1,128]{1,0:T(1,128)S(1)}, f32[1,128]{1,0:T(1,128)S(1)}, u32[]{:S(2)}, u32[]{:S(2)}) collective-permute-start(f32[1,128]{1,0:T(1,128)S(1)} %get-tuple-element.104), channel_id=1, source_target_pairs={{64,0},{128,64},{192,128},{256,192},{320,256},{384,320},{448,384},... | collective-permute-start | bytes 1544 | tf_op jit(solution)/shard_map/ppermute | solution.py:22
  18.0 14.0 %collective-permute-start.2 = (f32[3,66,1]{2,1,0:T(8,128)S(1)}, f32[3,66,1]{2,1,0:T(8,128)S(1)}, u32[]{:S(2)}, u32[]{:S(2)}) collective-permute-start(f32[3,66,1]{2,1,0:T(8,128)S(1)} %get-tuple-element.34), channel_id=1, source_target_pairs={{0,1},{1,2},{2,3},{3,4},{4,5},{5,6},{6,7},{7,8},{8,9},{9,10},{10,1... | collective-permute-start | bytes 2384 | tf_op jit(solution)/shard_map/ppermute | solution.py:21
  21.1 10.9 %collective-permute-start.3 = (f32[3,66,1]{2,1,0:T(8,128)S(1)}, f32[3,66,1]{2,1,0:T(8,128)S(1)}, u32[]{:S(2)}, u32[]{:S(2)}) collective-permute-start(f32[3,66,1]{2,1,0:T(8,128)S(1)} %get-tuple-element.35), channel_id=1, source_target_pairs={{1,0},{2,1},{3,2},{4,3},{5,4},{6,5},{7,6},{8,7},{9,8},{10,9},{11,1... | collective-permute-start | bytes 2384 | tf_op jit(solution)/shard_map/ppermute | solution.py:22
  28.6 8.0 %collective-permute-start.7 = (f32[66,1]{1,0:T(8,128)S(1)}, f32[66,1]{1,0:T(8,128)S(1)}, u32[]{:S(2)}, u32[]{:S(2)}) collective-permute-start(f32[66,1]{1,0:T(8,128)S(1)} %get-tuple-element.59), channel_id=1, source_target_pairs={{0,1},{1,2},{2,3},{3,4},{4,5},{5,6},{6,7},{7,8},{8,9},{9,10},{10,1... | collective-permute-start | bytes 800 | tf_op jit(solution)/shard_map/ppermute | solution.py:21
  48.5 8.0 %collective-permute-start.11 = (f32[66,1]{1,0:T(8,128)S(1)}, f32[66,1]{1,0:T(8,128)S(1)}, u32[]{:S(2)}, u32[]{:S(2)}) collective-permute-start(f32[66,1]{1,0:T(8,128)S(1)} %get-tuple-element.57), channel_id=1, source_target_pairs={{0,1},{1,2},{2,3},{3,4},{4,5},{5,6},{6,7},{7,8},{8,9},{9,10},{10,1... | collective-permute-start | bytes 800 | tf_op jit(solution)/shard_map/ppermute | solution.py:21
  56.7 9.3 %collective-permute-start.12 = (f32[1,128]{1,0:T(1,128)S(1)}, f32[1,128]{1,0:T(1,128)S(1)}, u32[]{:S(2)}, u32[]{:S(2)}) collective-permute-start(f32[1,128]{1,0:T(1,128)S(1)} %get-tuple-element.101), channel_id=1, source_target_pairs={{0,64},{64,128},{128,192},{192,256},{256,320},{320,384},{384,448},... | collective-permute-start | bytes 1544 | tf_op jit(solution)/shard_map/ppermute | solution.py:21
  68.0 8.0 %collective-permute-start.15 = (f32[66,1]{1,0:T(8,128)S(1)}, f32[66,1]{1,0:T(8,128)S(1)}, u32[]{:S(2)}, u32[]{:S(2)}) collective-permute-start(f32[66,1]{1,0:T(8,128)S(1)} %get-tuple-element.55), channel_id=1, source_target_pairs={{0,1},{1,2},{2,3},{3,4},{4,5},{5,6},{6,7},{7,8},{8,9},{9,10},{10,1... | collective-permute-start | bytes 800 | tf_op jit(solution)/shard_map/ppermute | solution.py:21
  90.3 7.8 collective-permute-start.19
  108.2 7.8 collective-permute-start.23
  207.7 27.6 %collective-permute-start.24 = (f32[1,32]{1,0:T(1,128)S(1)}, f32[1,32]{1,0:T(1,128)S(1)}, u32[]{:S(2)}, u32[]{:S(2)}) collective-permute-start(f32[1,32]{1,0:T(1,128)S(1)} %get-tuple-element.169), channel_id=1, source_target_pairs={{0,64},{64,128},{128,192},{192,256},{256,320},{320,384},{384,448},... | collective-permute-start | bytes 392 | tf_op jit(solution)/shard_map/ppermute | solution.py:21
  242.1 7.8 collective-permute-start.27
  269.2 20.5 %all-to-all-start = ((f32[64,1,128]{2,1,0:T(1,128)}), f32[64,1,128]{2,1,0:T(1,128)S(1)}, u32[]{:S(2)}, u32[]{:S(2)}) async-start(f32[64,1,128]{2,1,0:T(1,128)} %reshape.136), calls=%async_computation | async-start | bytes 65536 | tf_op jit(solution)/shard_map/all_to_all | solution.py:123
  291.2 20.5 %collective-permute-start.32 = (f32[1,1024]{1,0:T(1,128)S(1)}, f32[1,1024]{1,0:T(1,128)S(1)}, u32[]{:S(2)}, u32[]{:S(2)}) collective-permute-start(f32[1,1024]{1,0:T(1,128)S(1)} %get-tuple-element.97), channel_id=1, source_target_pairs={{0,64},{64,128},{128,192},{192,256},{256,320},{320,384},{384,448},... | collective-permute-start | bytes 12296 | tf_op jit(solution)/shard_map/ppermute | solution.py:21
  295.7 16.0 %collective-permute-start.33 = (f32[1,1024]{1,0:T(1,128)S(1)}, f32[1,1024]{1,0:T(1,128)S(1)}, u32[]{:S(2)}, u32[]{:S(2)}) collective-permute-start(f32[1,1024]{1,0:T(1,128)S(1)} %get-tuple-element.96), channel_id=1, source_target_pairs={{64,0},{128,64},{192,128},{256,192},{320,256},{384,320},{448,384},... | collective-permute-start | bytes 12296 | tf_op jit(solution)/shard_map/ppermute | solution.py:22
  364.3 7.8 collective-permute-start.43
  400.6 7.8 collective-permute-start.51
  418.8 7.8 collective-permute-start.55
  437.0 8.0 %collective-permute-start.59 = (f32[66,1]{1,0:T(8,128)S(1)}, f32[66,1]{1,0:T(8,128)S(1)}, u32[]{:S(2)}, u32[]{:S(2)}) collective-permute-start(f32[66,1]{1,0:T(8,128)S(1)} %get-tuple-element.53), channel_id=1, source_target_pairs={{0,1},{1,2},{2,3},{3,4},{4,5},{5,6},{6,7},{7,8},{8,9},{9,10},{10,1... | collective-permute-start | bytes 800 | tf_op jit(solution)/shard_map/ppermute | solution.py:21
  455.3 8.0 %collective-permute-start.63 = (f32[66,1]{1,0:T(8,128)S(1)}, f32[66,1]{1,0:T(8,128)S(1)}, u32[]{:S(2)}, u32[]{:S(2)}) collective-permute-start(f32[66,1]{1,0:T(8,128)S(1)} %get-tuple-element.51), channel_id=1, source_target_pairs={{0,1},{1,2},{2,3},{3,4},{4,5},{5,6},{6,7},{7,8},{8,9},{9,10},{10,1... | collective-permute-start | bytes 800 | tf_op jit(solution)/shard_map/ppermute | solution.py:21
  473.5 8.0 %collective-permute-start.67 = (f32[66,1]{1,0:T(8,128)S(1)}, f32[66,1]{1,0:T(8,128)S(1)}, u32[]{:S(2)}, u32[]{:S(2)}) collective-permute-start(f32[66,1]{1,0:T(8,128)S(1)} %get-tuple-element.49), channel_id=1, source_target_pairs={{0,1},{1,2},{2,3},{3,4},{4,5},{5,6},{6,7},{7,8},{8,9},{9,10},{10,1... | collective-permute-start | bytes 800 | tf_op jit(solution)/shard_map/ppermute | solution.py:21
  491.6 8.0 %collective-permute-start.71 = (f32[66,1]{1,0:T(8,128)S(1)}, f32[66,1]{1,0:T(8,128)S(1)}, u32[]{:S(2)}, u32[]{:S(2)}) collective-permute-start(f32[66,1]{1,0:T(8,128)S(1)} %get-tuple-element.47), channel_id=1, source_target_pairs={{0,1},{1,2},{2,3},{3,4},{4,5},{5,6},{6,7},{7,8},{8,9},{9,10},{10,1... | collective-permute-start | bytes 800 | tf_op jit(solution)/shard_map/ppermute | solution.py:21
  509.8 8.0 %collective-permute-start.75 = (f32[66,1]{1,0:T(8,128)S(1)}, f32[66,1]{1,0:T(8,128)S(1)}, u32[]{:S(2)}, u32[]{:S(2)}) collective-permute-start(f32[66,1]{1,0:T(8,128)S(1)} %get-tuple-element.45), channel_id=1, source_target_pairs={{0,1},{1,2},{2,3},{3,4},{4,5},{5,6},{6,7},{7,8},{8,9},{9,10},{10,1... | collective-permute-start | bytes 800 | tf_op jit(solution)/shard_map/ppermute | solution.py:21
  530.4 7.8 collective-permute-start.79
  548.4 7.8 collective-permute-start.83
  585.0 7.8 collective-permute-start.91
  671.4 7.8 collective-permute-start.103
  707.7 7.8 collective-permute-start.111
  725.9 7.8 collective-permute-start.115
  744.1 8.0 %collective-permute-start.119 = (f32[66,1]{1,0:T(8,128)S(1)}, f32[66,1]{1,0:T(8,128)S(1)}, u32[]{:S(2)}, u32[]{:S(2)}) collective-permute-start(f32[66,1]{1,0:T(8,128)S(1)} %get-tuple-element.43), channel_id=1, source_target_pairs={{0,1},{1,2},{2,3},{3,4},{4,5},{5,6},{6,7},{7,8},{8,9},{9,10},{10,1... | collective-permute-start | bytes 800 | tf_op jit(solution)/shard_map/ppermute | solution.py:21
  762.4 8.0 %collective-permute-start.123 = (f32[66,1]{1,0:T(8,128)S(1)}, f32[66,1]{1,0:T(8,128)S(1)}, u32[]{:S(2)}, u32[]{:S(2)}) collective-permute-start(f32[66,1]{1,0:T(8,128)S(1)} %get-tuple-element.41), channel_id=1, source_target_pairs={{0,1},{1,2},{2,3},{3,4},{4,5},{5,6},{6,7},{7,8},{8,9},{9,10},{10,1... | collective-permute-start | bytes 800 | tf_op jit(solution)/shard_map/ppermute | solution.py:21
  780.6 8.0 %collective-permute-start.127 = (f32[66,1]{1,0:T(8,128)S(1)}, f32[66,1]{1,0:T(8,128)S(1)}, u32[]{:S(2)}, u32[]{:S(2)}) collective-permute-start(f32[66,1]{1,0:T(8,128)S(1)} %get-tuple-element.39), channel_id=1, source_target_pairs={{0,1},{1,2},{2,3},{3,4},{4,5},{5,6},{6,7},{7,8},{8,9},{9,10},{10,1... | collective-permute-start | bytes 800 | tf_op jit(solution)/shard_map/ppermute | solution.py:21
  (109 other events, 1101.8 us)
